TPU v7x, 512 devices: a whole 4x8x8 slice. The times are simulated.
512 devices in a mesh: samp: 64 (over z, x, core), var: 8 (over y).
Axes of the slice: x: 4, y: 8, z: 8, core: 2. Of those that a mesh axis runs over, the one named last changes fastest.
Arguments:
- genotypes: bfloat16 [65536, 12288], P('samp', 'var'), may hold values from 0 to 2, as said below
- start_q: float32 [64, 65536], P(None, 'samp'), may hold values from 0 to 1, as said below
Outputs:
- final_q: float32 [64, 65536], P(None, 'samp')
- final_p: float32 [64, 12288], P(None, 'var')
Inputs may be any that keep to these rules, and one draw needn't show every extreme that they name: `genotypes`: genotype counts, whole numbers. `start_q`: nonnegative proportions.
All inputs are finite; a program needn't handle non-finite values.
Results may differ from a plain program's by a relative error of at most 0.001.
Values sent between devices are 32-bit elements; how exact they have to be, the bound alone decides.
A program may use at most 64 MiB of HBM per device.

v0:
```python
import jax
import jax.numpy as jnp
from jax import lax
from jax.sharding import Mesh
from jax.sharding import PartitionSpec as P

ITERS = 2
SAMP = ("samp_0", "samp_1", "samp_2")


ridge_term = 1.0


def filled_up(lines, length):
    spare = -lines.shape[0] % length
    if not spare:
        return lines
    return jnp.concatenate([lines, jnp.zeros((spare, *lines.shape[1:]), lines.dtype)])


def copy_for_each(x, axis):
    copies = jnp.broadcast_to(x, (lax.axis_size(axis), *x.shape))
    return lax.all_to_all(copies, axis, split_axis=0, concat_axis=0, tiled=True)


def joined_along(parts, dim):
    lengths = list(parts.shape[1:])
    lengths[dim] *= parts.shape[0]
    return jnp.moveaxis(parts, 0, dim).reshape(lengths)


def gather_axes(x, axes, dim):
    far, near = axes
    parts = copy_for_each(copy_for_each(x, far), near)
    return joined_along(parts.swapaxes(0, 1).reshape(-1, *x.shape), dim)


def in_blocks(x, dim, length):
    lengths = x.shape
    parts = x.reshape(*lengths[:dim], length, lengths[dim] // length, *lengths[dim + 1 :])
    return jnp.moveaxis(parts, dim, 0)


def sent_and_summed(x, axis, dim):
    length = lax.axis_size(axis)
    parts = lax.all_to_all(in_blocks(x, dim, length), axis, 0, 0, tiled=True)
    return jnp.sum(parts, axis=0)


def sum_in_two_steps(x, axes, dim):
    far, near = axes
    parts = in_blocks(x, dim, lax.axis_size(far))
    nearer = sent_and_summed(parts, near, dim + 1)
    arrived = lax.all_to_all(nearer, far, split_axis=0, concat_axis=0, tiled=True)
    return arrived.sum(axis=0)


def sum_by_parts(x, axes):
    lines = x.reshape(-1, x.shape[-1])
    padded = filled_up(lines, lax.axis_size(axes[0]) * lax.axis_size(axes[1]))
    whole = gather_axes(sum_in_two_steps(padded, axes, 0), axes, 0)
    return lax.slice_in_dim(whole, 0, len(lines)).reshape(x.shape)


def of_everyone(x, axis):
    return copy_for_each(x, axis).sum(axis=0)


def collect(x, axis, dim):
    return joined_along(copy_for_each(x, axis), dim)


def gram_solve(gram_matrix, right_side):
    eye_matrix = jnp.eye(gram_matrix.shape[0], dtype=jnp.float32)
    factor_low = jnp.linalg.cholesky(gram_matrix + ridge_term * eye_matrix)
    return jax.scipy.linalg.cho_solve((factor_low, True), right_side)


def body(genotypes, start_q):
    halved = genotypes * jnp.asarray(0.5, dtype=genotypes.dtype)
    ancestry = start_q
    frequency = None
    for iteration in range(ITERS):
        ancestry_b = ancestry.astype(jnp.bfloat16)
        cross_part = jnp.dot(ancestry_b, halved, preferred_element_type=jnp.float32)
        gram_part = jnp.dot(ancestry, ancestry.T, precision=lax.Precision.HIGHEST)
        width = cross_part.shape[1]
        summed = sum_by_parts(
            jnp.concatenate([cross_part, gram_part], axis=1), (("samp_0", "samp_1"), "samp_2")
        )
        frequency = gram_solve(summed[:, width:], summed[:, :width])
        freq_b = frequency.astype(jnp.bfloat16)
        sample_part = lax.dot_general(
            freq_b, halved, (((1,), (1,)), ((), ())), preferred_element_type=jnp.float32
        )
        pgram_part = jnp.dot(frequency, frequency.T, precision=lax.Precision.HIGHEST)
        sample_share = sent_and_summed(sample_part, "var", 1)
        gram_p = of_everyone(pgram_part, "var")
        ancestry_share = gram_solve(gram_p, sample_share)
        ancestry = collect(ancestry_share, "var", 1)
    return (ancestry, frequency)


def solution(mesh):
    finer = Mesh(
        mesh.devices.reshape(8, 4, 2, mesh.shape["var"]), ("samp_0", "samp_1", "samp_2", "var")
    )
    return jax.shard_map(
        body,
        mesh=finer,
        in_specs=(P(SAMP, "var"), P(None, SAMP)),
        out_specs=(P(None, SAMP), P(None, "var")),
        check_vma=False,
    )
```

profile of v0, /device:TPU:1, one launch (start us, length us, event | category | flops | bytes accessed | tf_op | source)
XLA Modules:
  0.0 248.0 jit_solution(5854194492004891408)
XLA Ops:
  2.0 2.7 %convolution_bitcast_fusion = f32[64,1536]{1,0:T(8,128)S(1)} fusion(bf16[1024,1536]{1,0:T(8,128)(2,1)} %param.7, f32[64,1024]{1,0:T(8,128)} %param.8), kind=kOutput, calls=%fused_computation | convolution fusion | flops 202964992 | bytes 3801088 | tf_op jit(solution)/shard_map/dot_general | solution.py:85
  5.0 10.6 %all_to_all.76 = f32[2,32,1,1600]{3,1,2,0:T(8,128)S(1)} all-to-all(f32[2,32,1,1600]{3,1,2,0:T(8,128)S(1)} %bitcast.115), channel_id=1, replica_groups=mesh['samp_0'=8,'samp_1'=4,'samp_2'=2,'var'=8] {'samp_2'}, dimensions={0} | all-to-all | bytes 819200 | tf_op jit(solution)/shard_map/all_to_all | solution.py:46
  15.8 18.1 %all_to_all.77 = f32[32,1,1600]{2,1,0:T(1,128)S(1)} all-to-all(f32[32,1,1600]{2,1,0:T(1,128)S(1)} %reduce_sum.77), channel_id=1, replica_groups=mesh['samp_0'=8,'samp_1'=4,'samp_2'=2,'var'=8] {'samp_0','samp_1'}, dimensions={0} | all-to-all | bytes 409600 | tf_op jit(solution)/shard_map/all_to_all | solution.py:54
  34.1 14.1 %all_to_all.78 = f32[32,1,1600]{2,1,0:T(1,128)S(1)} all-to-all(f32[32,1,1600]{2,1,0:T(1,128)S(1)} %broadcast_in_dim.25), channel_id=1, replica_groups=mesh['samp_0'=8,'samp_1'=4,'samp_2'=2,'var'=8] {'samp_0','samp_1'}, dimensions={0} | all-to-all | bytes 409600 | tf_op jit(solution)/shard_map/all_to_all | solution.py:23
  48.2 7.1 %all_to_all.79 = f32[2,32,1,1600]{3,1,2,0:T(8,128)S(1)} all-to-all(f32[2,32,1,1600]{3,1,2,0:T(8,128)S(1)} %broadcast_in_dim.26), channel_id=1, replica_groups=mesh['samp_0'=8,'samp_1'=4,'samp_2'=2,'var'=8] {'samp_2'}, dimensions={0} | all-to-all | bytes 819200 | tf_op jit(solution)/shard_map/all_to_all | solution.py:23
  56.5 2.1 reshape_reshape.13
  59.5 5.8 %cholesky.74 = f32[64,64]{1,0:T(8,128)S(1)} custom-call(f32[64,64]{1,0:T(8,128)S(1)} %fusion.49), custom_call_target="Cholesky" | custom-call | tf_op jit(solution)/shard_map/jit(cholesky)/cholesky | solution.py:75
  66.7 4.9 %custom-call.14 = f32[1,64,64]{1,2,0:T(8,128)S(1)} custom-call(f32[1,64,64]{2,1,0:T(8,128)S(1)} %fusion.28), custom_call_target="InvertDiagBlocksLowerTriangular" | custom-call | tf_op jit(solution)/shard_map/jit(_cho_solve)/triangular_solve | solution.py:76
  76.1 1.8 reshape.44
  77.9 6.8 %all-to-all-start.4 = ((f32[8,1,4096]{2,1,0:T(1,128)}), f32[8,1,4096]{2,1,0:T(1,128)}, u32[]{:S(2)}, u32[]{:S(2)}) async-start(f32[8,1,4096]{2,1,0:T(1,128)} %reshape.44), calls=%async_computation.4 | async-start | bytes 262144 | tf_op jit(solution)/shard_map/all_to_all | solution.py:23
  86.5 6.2 %all-to-all-done.4 = f32[8,1,4096]{2,1,0:T(1,128)} async-done(((f32[8,1,4096]{2,1,0:T(1,128)}), f32[8,1,4096]{2,1,0:T(1,128)}, u32[]{:S(2)}, u32[]{:S(2)}) %all-to-all-start.4) | async-done | bytes 131104 | tf_op jit(solution)/shard_map/all_to_all | solution.py:23
  92.7 4.0 %all-to-all-start.5 = ((f32[8,64,128]{2,1,0:T(8,128)}), f32[8,64,128]{2,1,0:T(8,128)}, u32[]{:S(2)}, u32[]{:S(2)}) async-start(f32[8,64,128]{2,1,0:T(8,128)} %bitcast.112), calls=%async_computation.5 | async-start | bytes 524288 | tf_op jit(solution)/shard_map/all_to_all | solution.py:46
  97.3 1.8 reduce.8
  99.5 5.8 %cholesky.85 = f32[64,64]{1,0:T(8,128)S(1)} custom-call(f32[64,64]{1,0:T(8,128)S(1)} %fusion.45), custom_call_target="Cholesky" | custom-call | tf_op jit(solution)/shard_map/jit(cholesky)/cholesky | solution.py:75
  106.7 4.9 %custom-call.15 = f32[1,64,64]{1,2,0:T(8,128)S(1)} custom-call(f32[1,64,64]{2,1,0:T(8,128)S(1)} %fusion.29), custom_call_target="InvertDiagBlocksLowerTriangular" | custom-call | tf_op jit(solution)/shard_map/jit(_cho_solve)/triangular_solve | solution.py:76
  113.0 15.7 %all_to_all.80 = f32[8,64,128]{2,1,0:T(8,128)S(1)} all-to-all(f32[8,64,128]{2,1,0:T(8,128)S(1)} %broadcast_in_dim.28), channel_id=1, replica_groups=mesh['samp_0'=8,'samp_1'=4,'samp_2'=2,'var'=8] {'var'}, dimensions={0} | all-to-all | bytes 524288 | tf_op jit(solution)/shard_map/all_to_all | solution.py:23
  130.6 2.0 reshape_reshape.14
  133.6 8.2 %all_to_all.81 = f32[2,32,1,1600]{3,1,2,0:T(8,128)} all-to-all(f32[2,32,1,1600]{3,1,2,0:T(8,128)S(1)} %bitcast.117), channel_id=1, replica_groups=mesh['samp_0'=8,'samp_1'=4,'samp_2'=2,'var'=8] {'samp_2'}, dimensions={0} | all-to-all | bytes 819200 | tf_op jit(solution)/shard_map/all_to_all | solution.py:46
  143.0 13.9 %all_to_all.82 = f32[32,1,1600]{2,1,0:T(1,128)S(1)} all-to-all(f32[32,1,1600]{2,1,0:T(1,128)S(1)} %reduce_sum.82), channel_id=1, replica_groups=mesh['samp_0'=8,'samp_1'=4,'samp_2'=2,'var'=8] {'samp_0','samp_1'}, dimensions={0} | all-to-all | bytes 409600 | tf_op jit(solution)/shard_map/all_to_all | solution.py:54
  157.2 14.1 %all_to_all.83 = f32[32,1,1600]{2,1,0:T(1,128)S(1)} all-to-all(f32[32,1,1600]{2,1,0:T(1,128)S(1)} %broadcast_in_dim.29), channel_id=1, replica_groups=mesh['samp_0'=8,'samp_1'=4,'samp_2'=2,'var'=8] {'samp_0','samp_1'}, dimensions={0} | all-to-all | bytes 409600 | tf_op jit(solution)/shard_map/all_to_all | solution.py:23
  171.4 6.9 %all_to_all.84 = f32[2,32,1,1600]{3,1,2,0:T(8,128)S(1)} all-to-all(f32[2,32,1,1600]{3,1,2,0:T(8,128)S(1)} %broadcast_in_dim.30), channel_id=1, replica_groups=mesh['samp_0'=8,'samp_1'=4,'samp_2'=2,'var'=8] {'samp_2'}, dimensions={0} | all-to-all | bytes 819200 | tf_op jit(solution)/shard_map/all_to_all | solution.py:23
  179.3 2.1 reshape_reshape.15
  182.3 5.8 %cholesky.96 = f32[64,64]{1,0:T(8,128)S(1)} custom-call(f32[64,64]{1,0:T(8,128)S(1)} %fusion.40), custom_call_target="Cholesky" | custom-call | tf_op jit(solution)/shard_map/jit(cholesky)/cholesky | solution.py:75
  189.5 4.9 %custom-call.16 = f32[1,64,64]{1,2,0:T(8,128)S(1)} custom-call(f32[1,64,64]{2,1,0:T(8,128)S(1)} %fusion.30), custom_call_target="InvertDiagBlocksLowerTriangular" | custom-call | tf_op jit(solution)/shard_map/jit(_cho_solve)/triangular_solve | solution.py:76
  199.0 1.8 reshape.46
  200.8 4.0 %all-to-all-start.11 = ((f32[8,1,4096]{2,1,0:T(1,128)}), f32[8,1,4096]{2,1,0:T(1,128)}, u32[]{:S(2)}, u32[]{:S(2)}) async-start(f32[8,1,4096]{2,1,0:T(1,128)} %reshape.46), calls=%async_computation.11 | async-start | bytes 262144 | tf_op jit(solution)/shard_map/all_to_all | solution.py:23
  206.6 6.6 %all-to-all-done.11 = f32[8,1,4096]{2,1,0:T(1,128)} async-done(((f32[8,1,4096]{2,1,0:T(1,128)}), f32[8,1,4096]{2,1,0:T(1,128)}, u32[]{:S(2)}, u32[]{:S(2)}) %all-to-all-start.11) | async-done | bytes 131104 | tf_op jit(solution)/shard_map/all_to_all | solution.py:23
  213.2 3.4 %all-to-all-start.12 = ((f32[8,64,128]{2,1,0:T(8,128)}), f32[8,64,128]{2,1,0:T(8,128)S(1)}, u32[]{:S(2)}, u32[]{:S(2)}) async-start(f32[8,64,128]{2,1,0:T(8,128)} %bitcast.110), calls=%async_computation.12 | async-start | bytes 524288 | tf_op jit(solution)/shard_map/all_to_all | solution.py:46
  216.6 1.9 reduce.9
  218.8 5.8 %cholesky.107 = f32[64,64]{1,0:T(8,128)S(1)} custom-call(f32[64,64]{1,0:T(8,128)S(1)} %fusion.36), custom_call_target="Cholesky" | custom-call | tf_op jit(solution)/shard_map/jit(cholesky)/cholesky | solution.py:75
  226.1 4.9 %custom-call.17 = f32[1,64,64]{1,2,0:T(8,128)S(1)} custom-call(f32[1,64,64]{2,1,0:T(8,128)S(1)} %fusion.31), custom_call_target="InvertDiagBlocksLowerTriangular" | custom-call | tf_op jit(solution)/shard_map/jit(_cho_solve)/triangular_solve | solution.py:76
  231.5 15.8 %all_to_all.85 = f32[8,64,128]{2,1,0:T(8,128)S(1)} all-to-all(f32[8,64,128]{2,1,0:T(8,128)S(1)} %broadcast_in_dim.32), channel_id=1, replica_groups=mesh['samp_0'=8,'samp_1'=4,'samp_2'=2,'var'=8] {'var'}, dimensions={0} | all-to-all | bytes 524288 | tf_op jit(solution)/shard_map/all_to_all | solution.py:23
  (88 shorter events, 32.4 us)
Async XLA Ops:
  48.2 36.5 %copy-start = (bf16[1024,1536]{1,0:T(8,128)(2,1)S(1)}, bf16[1024,1536]{1,0:T(8,128)(2,1)}, u32[]{:S(2)}) copy-start(bf16[1024,1536]{1,0:T(8,128)(2,1)} %param.7) | copy-start | bytes 9437188
  71.5 0.6 copy-start.2
  77.9 14.8 %all-to-all-start.4 = ((f32[8,1,4096]{2,1,0:T(1,128)}), f32[8,1,4096]{2,1,0:T(1,128)}, u32[]{:S(2)}, u32[]{:S(2)}) async-start(f32[8,1,4096]{2,1,0:T(1,128)} %reshape.44), calls=%async_computation.4 | async-start | bytes 262144 | tf_op jit(solution)/shard_map/all_to_all | solution.py:23
  92.7 18.9 %all-to-all-start.5 = ((f32[8,64,128]{2,1,0:T(8,128)}), f32[8,64,128]{2,1,0:T(8,128)}, u32[]{:S(2)}, u32[]{:S(2)}) async-start(f32[8,64,128]{2,1,0:T(8,128)} %bitcast.112), calls=%async_computation.5 | async-start | bytes 524288 | tf_op jit(solution)/shard_map/all_to_all | solution.py:46
  194.4 0.6 copy-start.3
  197.8 15.4 %copy-start.1 = (f32[64,1536]{1,0:T(8,128)}, f32[64,1536]{1,0:T(8,128)S(1)}, u32[]{:S(2)}) copy-start(f32[64,1536]{1,0:T(8,128)S(1)} %fusion.37) | copy-start | bytes 1179652
  200.8 12.4 %all-to-all-start.11 = ((f32[8,1,4096]{2,1,0:T(1,128)}), f32[8,1,4096]{2,1,0:T(1,128)}, u32[]{:S(2)}, u32[]{:S(2)}) async-start(f32[8,1,4096]{2,1,0:T(1,128)} %reshape.46), calls=%async_computation.11 | async-start | bytes 262144 | tf_op jit(solution)/shard_map/all_to_all | solution.py:23
  213.2 17.8 %all-to-all-start.12 = ((f32[8,64,128]{2,1,0:T(8,128)}), f32[8,64,128]{2,1,0:T(8,128)S(1)}, u32[]{:S(2)}, u32[]{:S(2)}) async-start(f32[8,64,128]{2,1,0:T(8,128)} %bitcast.110), calls=%async_computation.12 | async-start | bytes 524288 | tf_op jit(solution)/shard_map/all_to_all | solution.py:46
where the time goes:
time: 250 us; the launch traced here: 248 us
  blocking collectives  124 us (50%)
  other arithmetic  55.4 us (22%)
  local copies, waits for them, and re-layouts  21.5 us (9%)
  starting transfers between devices  18.3 us (7%)
  matrix products  14.4 us (6%)
  waiting for transfers between devices  12.8 us (5%)
    all_to_all x6, blocking collectives, copy_for_each(): return lax.all_to_all(copies, axis, split_axis=0, concat_axis=0, tiled=True)  73.7 us
    all_to_all x2, blocking collectives, sum_in_two_steps(): lax.all_to_all(nearer, far, split_axis=0, concat_axis=0, tiled=True)  32 us
    another operation x12, other arithmetic, gram_solve(): factor_low = jnp.linalg.cholesky(gram_matrix + ridge_term * eye_matrix)  26.2 us
    another operation x8, other arithmetic, gram_solve(): return jax.scipy.linalg.cho_solve((factor_low, True), right_side)  22.2 us
    all_to_all x2, blocking collectives, sent_and_summed(): parts = lax.all_to_all(in_blocks(x, dim, length), axis, 0, 0, tiled=True)  18.8 us
    all_to_all x2, waiting for transfers between devices, copy_for_each(): return lax.all_to_all(copies, axis, split_axis=0, concat_axis=0, tiled=True)  12.8 us
    all_to_all x2, starting transfers between devices, copy_for_each(): return lax.all_to_all(copies, axis, split_axis=0, concat_axis=0, tiled=True)  10.8 us
    all_to_all x2, starting transfers between devices, sent_and_summed(): parts = lax.all_to_all(in_blocks(x, dim, length), axis, 0, 0, tiled=True)  7.46 us
  transfers between devices with their start and end apart: 4, of which 2 were waited for; matrix products, arithmetic and copies ran while one was open for 13% of the time, Pallas kernels for 0%

commit v1 on v0

v1 whole, which is shorter than its diff:
```python
import jax
import jax.numpy as jnp
from jax import lax
from jax.experimental import pallas as pl
from jax.experimental.pallas import tpu as pltpu
from jax.sharding import Mesh
from jax.sharding import PartitionSpec as P

ITERS = 2
RIDGE = 1.0
K = 64
NZ, NX, NC, NY = 8, 4, 2, 8
S, V = 1024, 1536
SH, VH, VQ = S // 2, V // 2, V // 4
CROSS = 24
TILES = (CROSS + 4, CROSS)
ROWS = (40, 32)
EXACT = lax.Precision.HIGHEST
f32, bf16 = jnp.float32, jnp.bfloat16
MESH = pl.DeviceIdType.MESH


def dot(a, b, precision=None):
    return jnp.dot(a, b, precision=precision, preferred_element_type=f32)


def dot_t(a, b, precision=None):
    return lax.dot_general(
        a, b, (((1,), (1,)), ((), ())), precision=precision, preferred_element_type=f32
    )


def inverse(gram):
    row = lax.broadcasted_iota(jnp.int32, (K, 128), 0)
    lane = lax.broadcasted_iota(jnp.int32, (K, 128), 1)
    m = jnp.where(lane < K, gram + jnp.where(lane == row, RIDGE, 0.0), jnp.where(lane - K == row, 1.0, 0.0))
    sub = lax.broadcasted_iota(jnp.int32, (8, 128), 0)
    for b in range(0, K, 8):
        r = m[b : b + 8, :]
        cs = [jnp.broadcast_to(r[:, b + j : b + j + 1], (8, 128)) for j in range(8)]
        for j in range(8):
            c = cs[j]
            inv = 1.0 / c[j : j + 1, :]
            hit = sub == j
            rn = r[j : j + 1, :] * inv
            r = jnp.where(hit, rn, r - c * rn)
            for i in range(j + 1, 8):
                q = cs[i][j : j + 1, :] * inv
                cs[i] = jnp.where(hit, q, cs[i] - c * q)
        upd = m
        for j in range(8):
            upd = upd - m[:, b + j : b + j + 1] * r[j : j + 1, :]
        parts = ([upd[:b]] if b else []) + [r] + ([upd[b + 8 :]] if b + 8 < K else [])
        m = jnp.concatenate(parts, axis=0)
    return m[:, K:]


def far_first(k, n):
    half = (k + 1) // 2
    return n // 2 + half * (1 - 2 * (k % 2))


def kernel(
    g_ref, q_ref, qo_ref, po_ref,
    x, a, p, acc, qacc, gq, gacc, gbuf,
    cs0, cs1, cr0, cr1, t0, t1, r0, r1, f0, f1, fs0, fs1,
    qs0, qs1, qr0, qr1, qf0, qf1,
    load_sem, out_sem, core_s, core_r, rs_s, rs_r, ag_s, ag_r, cag_s, cag_r, ys_s, ys_r, yg_s, yg_r,
):
    z, xx, c, y = (lax.axis_index(n) for n in ("z", "x", "core", "var"))
    chip = z * NX + xx
    cs, cr, t, r, f, fs = (cs0, cs1), (cr0, cr1), (t0, t1), (r0, r1), (f0, f1), (fs0, fs1)
    qs, qr, qf = (qs0, qs1), (qr0, qr1), (qf0, qf1)
    sibling = {"core": 1 - c}
    lane = lax.broadcasted_iota(jnp.int32, (32, 128), 1)

    j_mine = (xx - z + 2 * NX - 1) % NX
    crossing = j_mine < 3
    even = z % 2 == 0
    owner = (crossing | even, crossing)
    mine = (jnp.where(crossing, 3 * z + j_mine, CROSS + z // 2), 3 * z + j_mine)

    def remote(src, dst, s_sem, r_sem, to):
        return pltpu.make_async_remote_copy(
            src_ref=src, dst_ref=dst, send_sem=s_sem, recv_sem=r_sem, device_id=to, device_id_type=MESH
        )

    def settle(ref, sem):
        pltpu.make_async_copy(ref, ref, sem).wait()

    loads = [
        pltpu.make_async_copy(q_ref, a, load_sem.at[0]),
        pltpu.make_async_copy(g_ref.at[pl.ds(0, SH)], x.at[pl.ds(0, SH)], load_sem.at[1]),
        pltpu.make_async_copy(g_ref.at[pl.ds(SH, SH)], x.at[pl.ds(SH, SH)], load_sem.at[2]),
    ]
    for load in loads:
        load.start()

    barrier = pltpu.get_barrier_semaphore()

    def greet(i, carry):
        to = {"z": (z + i // NX) % NZ, "x": (xx + i % NX) % NX}
        pl.semaphore_signal(barrier, inc=1, device_id=to, device_id_type=MESH)
        return carry

    lax.fori_loop(1, NZ * NX, greet, 0)

    def greet_y(i, carry):
        pl.semaphore_signal(barrier, inc=1, device_id={"var": (y + i) % NY}, device_id_type=MESH)
        return carry

    lax.fori_loop(1, NY, greet_y, 0)
    pl.semaphore_signal(barrier, inc=1, device_id=sibling, device_id_type=MESH)

    def start_columns(h, who):
        return pl.multiple_of(h * VH + VQ * who, 128)

    def samples_part(k, exchange):
        block = a[:, k * SH : (k + 1) * SH]
        half = (block * 0.5).astype(bf16)
        gram = dot_t(block, block, EXACT)
        gq[:, :K] = gram if k == 0 else gq[:, :K] + gram
        for h in range(2):
            for who in (1 - c, c):
                cols = start_columns(h, who)
                part = dot(half, x[k * SH : (k + 1) * SH, pl.ds(cols, VQ)])
                if k:
                    part = part + acc[:, pl.ds(cols, VQ)]
                if not exchange:
                    acc[:, pl.ds(cols, VQ)] = part
                    continue
                out = cs[h] if who is not c else t[h]
                for l in range(3):
                    out[8 * l : 8 * l + 8] = part[:, 128 * l : 128 * l + 128].reshape(8, 8, 128)
                if h == 0:
                    first = pl.multiple_of(32 * who, 32)
                    out[CROSS : CROSS + 4] = gq[pl.ds(first, 32), :].reshape(4, 8, 128)
                if who is not c:
                    remote(cs[h], cr[h], core_s.at[h], core_r.at[h], sibling).start()

    def sum_over_samples(h):
        settle(cr[h], core_r.at[h])
        t[h][...] = t[h][...] + cr[h][...]

        def send(tile, to):
            remote(t[h].at[tile], r[h].at[chip], rs_s.at[h], rs_r.at[h], to).start()

        def cross(i, carry):
            zt = (z + far_first(i // 3, NZ)) % NZ
            j = i % 3
            xt = (zt + 1 + j) % NX

            @pl.when((zt != z) | (xt != xx))
            def _():
                send(3 * zt + j, {"z": zt, "x": xt})

            return carry

        lax.fori_loop(0, CROSS, cross, 0)
        if h == 0:

            def gram(i, carry):
                zt = 2 * i
                xt = zt % NX

                @pl.when((zt != z) | (xt != xx))
                def _():
                    send(CROSS + i, {"z": zt, "x": xt})

                return carry

            lax.fori_loop(0, 4, gram, 0)

    def spread_sums(h):
        @pl.when(owner[h])
        def _():
            settle(r[h].at[pl.ds(0, 31)], rs_r.at[h])
            r[h][chip] = t[h][mine[h]]
            f[h][mine[h]] = jnp.sum(r[h][...], axis=0)

            def send(i, carry):
                zt = (z + far_first(i // NX, NZ)) % NZ
                xt = (xx + far_first(i % NX, NX)) % NX
                tile = f[h].at[mine[h]]
                remote(tile, tile, ag_s.at[h], ag_r.at[h], {"z": zt, "x": xt}).start()
                return carry

            lax.fori_loop(0, NZ * NX - 1, send, 0)

    def to_sibling(h):
        n = TILES[h]

        @pl.when(owner[h])
        def _():
            settle(f[h].at[pl.ds(0, n - 1)], ag_r.at[h])

        @pl.when(jnp.logical_not(owner[h]))
        def _():
            settle(f[h], ag_r.at[h])

        remote(f[h], fs[h], cag_s.at[h], cag_r.at[h], sibling).start()

    def frequencies(h, ginv):
        for src, who in ((f[h], c), (fs[h], 1 - c)):
            if src is fs[h]:
                settle(fs[h], cag_r.at[h])
            total = jnp.concatenate([src[8 * l : 8 * l + 8].reshape(K, 128) for l in range(3)], axis=1)
            p[:, pl.ds(start_columns(h, who), VQ)] = dot(ginv, total, EXACT)

    def send_y(h):
        def send(i, carry):
            yt = (y + far_first(i, NY)) % NY
            remote(qs[h].at[yt], qr[h].at[y], ys_s.at[h], ys_r.at[h], {"var": yt}).start()
            return carry

        lax.fori_loop(0, NY - 1, send, 0)

    def variants_part(h):
        block = p[:, h * VH : (h + 1) * VH]
        half = (block * 0.5).astype(bf16)
        gram = dot_t(block, block, EXACT)
        if h == 0:
            gacc[:, :K] = gram
        else:
            gacc[:, :K] = gacc[:, :K] + gram
            qs[0][:, :8, :] = gacc[...].reshape(8, 8, 128)
        for k in range(2):
            for s in range(k * SH, (k + 1) * SH, 256):
                part = dot_t(half, x[s : s + 256, h * VH : (h + 1) * VH])
                if h == 0:
                    qacc[:, s : s + 256] = part
                    continue
                part = part + qacc[:, s : s + 256]
                for b in range(2):
                    top = part[:32, 128 * b : 128 * b + 128]
                    low = part[32:, 128 * b : 128 * b + 128]
                    peer = (s - k * SH) // 64 + 2 * b
                    at = ROWS[k] - 32
                    qs[k][peer, at:, :] = jnp.where(lane < K, top, pltpu.roll(low, K, 1))
                    qs[k][peer + 1, at:, :] = jnp.where(lane < K, pltpu.roll(top, K, 1), low)
            if h == 1:
                send_y(k)

    def spread_y(k):
        settle(qr[k].at[pl.ds(0, NY - 1)], ys_r.at[k])
        qr[k][y] = qs[k][y]
        qf[k][y] = jnp.sum(qr[k][...], axis=0)

        def send(i, carry):
            yt = (y + far_first(i, NY)) % NY
            mine_y = qf[k].at[y]
            remote(mine_y, mine_y, yg_s.at[k], yg_r.at[k], {"var": yt}).start()
            return carry

        lax.fori_loop(0, NY - 1, send, 0)

    def ancestries(k, hinv):
        at = ROWS[k] - 32
        blocks = []
        for m in range(4):
            one, two = qf[k][2 * m, at:, :], qf[k][2 * m + 1, at:, :]
            top = jnp.where(lane < K, one, pltpu.roll(two, K, 1))
            low = jnp.where(lane < K, pltpu.roll(one, K, 1), two)
            blocks.append(jnp.concatenate([top, low], axis=0))
        a[:, k * SH : (k + 1) * SH] = dot(hinv, jnp.concatenate(blocks, axis=1), EXACT)

    gq[...] = jnp.zeros_like(gq)
    gacc[...] = jnp.zeros_like(gacc)
    loads[0].wait()
    loads[1].wait()
    samples_part(0, False)
    loads[2].wait()
    pl.semaphore_wait(barrier, NZ * NX - 1 + NY - 1 + 1)
    samples_part(1, True)

    def iteration(it, carry):
        sum_over_samples(0)
        sum_over_samples(1)
        spread_sums(0)
        spread_sums(1)
        to_sibling(0)
        settle(fs[0], cag_r.at[0])
        gbuf[pl.ds(4 * c, 4)] = f[0][CROSS:]
        gbuf[pl.ds(4 * (1 - c), 4)] = fs[0][CROSS:]
        ginv = inverse(gbuf[...].reshape(K, 128))
        for src, who in ((f[0], c), (fs[0], 1 - c)):
            total = jnp.concatenate([src[8 * l : 8 * l + 8].reshape(K, 128) for l in range(3)], axis=1)
            p[:, pl.ds(start_columns(0, who), VQ)] = dot(ginv, total, EXACT)
        variants_part(0)
        to_sibling(1)
        frequencies(1, ginv)
        variants_part(1)
        spread_y(0)
        spread_y(1)
        settle(qf[0].at[pl.ds(0, NY - 1)], yg_r.at[0])
        hinv = inverse(qf[0][:, :8, :].reshape(K, 128))
        ancestries(0, hinv)

        for h in range(2):
            settle(cs[h], core_s.at[h])
            settle(fs[h], cag_s.at[h])
            settle(qs[h].at[pl.ds(0, NY - 1)], ys_s.at[h])
            settle(qf[h].at[pl.ds(0, NY - 1)], yg_s.at[h])

            @pl.when(owner[h])
            def _():
                settle(t[h].at[pl.ds(0, TILES[h] - 1)], rs_s.at[h])
                settle(r[h].at[pl.ds(0, 31)], ag_s.at[h])

            @pl.when(jnp.logical_not(owner[h]))
            def _():
                settle(t[h], rs_s.at[h])

        @pl.when(it < ITERS - 1)
        def _():
            samples_part(0, False)

        settle(qf[1].at[pl.ds(0, NY - 1)], yg_r.at[1])
        ancestries(1, hinv)

        @pl.when(it < ITERS - 1)
        def _():
            samples_part(1, True)

        return carry

    lax.fori_loop(0, ITERS, iteration, 0)
    out_p = pltpu.make_async_copy(p, po_ref, out_sem.at[0])
    out_q = pltpu.make_async_copy(a, qo_ref, out_sem.at[1])
    out_p.start()
    out_q.start()
    out_p.wait()
    out_q.wait()


def body(genotypes, start_q):
    def vm(*shape, dtype=f32):
        return pltpu.VMEM(shape, dtype)

    tiles = [vm(n, 8, 128) for n in TILES]
    chips = [vm(NZ * NX, 8, 128)] * 2
    along_y = [vm(NY, n, 128) for n in ROWS]
    sem = pltpu.SemaphoreType.DMA
    return pl.pallas_call(
        kernel,
        out_shape=(
            jax.ShapeDtypeStruct((K, S), f32),
            jax.ShapeDtypeStruct((K, V), f32),
        ),
        in_specs=[pl.BlockSpec(memory_space=pl.ANY)] * 2,
        out_specs=(pl.BlockSpec(memory_space=pl.ANY),) * 2,
        scratch_shapes=[
            vm(S, V, dtype=bf16), vm(K, S), vm(K, V), vm(K, V), vm(K, S), vm(K, 128), vm(K, 128), vm(8, 8, 128),
            *tiles, *tiles, *tiles, *chips, *tiles, *tiles,
            *along_y, *along_y, *along_y,
            sem((3,)), sem((2,)), *[sem((2,))] * 12,
        ],
        compiler_params=pltpu.CompilerParams(
            collective_id=0, has_side_effects=True, vmem_limit_bytes=48 * 2**20
        ),
    )(genotypes, start_q)


def solution(mesh):
    finer = Mesh(mesh.devices.reshape(NZ, NX, NC, NY), ("z", "x", "core", "var"))
    samp = ("z", "x", "core")
    return jax.shard_map(
        body,
        mesh=finer,
        in_specs=(P(samp, "var"), P(None, samp)),
        out_specs=(P(None, samp), P(None, "var")),
        check_vma=False,
    )
```

time: 250 us -> 99.9 us (0.40)
  blocking collectives: 124 us -> 0 us
  Pallas kernels: 0 us -> 94.8 us
  other arithmetic: 55.4 us -> 0 us
  starting transfers between devices: 18.3 us -> 0 us
  local copies, waits for them, and re-layouts: 21.5 us -> 4.28 us
  matrix products: 14.4 us -> 0 us
  waiting for transfers between devices: 12.8 us -> 0 us
    all_to_all x10 -> x0, blocking collectives: 124 us -> none  [the longest x6 73.7 us: copy_for_each(): return lax.all_to_all(copies, axis, split_axis=0, concat_axis=0, tiled=True)]
    pallas_call x0 -> x1, Pallas kernels: none -> 94.8 us  [body(): pl.pallas_call(kernel, out_shape=(jax.ShapeDtypeStruct((K, S), f32), jax....]
    another operation x20 -> x0, other arithmetic: 48.4 us -> none  [the longest x12 26.2 us: gram_solve(): factor_low = jnp.linalg.cholesky(gram_matrix + ridge_term * eye_matrix)]
    all_to_all x4 -> x0, starting transfers between devices: 18.3 us -> none  [the longest x2 10.8 us: copy_for_each(): return lax.all_to_all(copies, axis, split_axis=0, concat_axis=0, tiled=True)]
    all_to_all x4 -> x0, waiting for transfers between devices: 12.8 us -> none  [the longest x2 12.8 us: copy_for_each(): return lax.all_to_all(copies, axis, split_axis=0, concat_axis=0, tiled=True)]
    dot_general x8 -> x0, matrix products: 8.12 us -> none  [the longest x2 3.32 us: body(): cross_part = jnp.dot(ancestry_b, halved, preferred_element_type=jnp.float32)]
    another operation x6 -> x0, local copies, waits for them, and re-layouts: 7.43 us -> none  [the longest x2 4.11 us: joined_along(): return jnp.moveaxis(parts, 0, dim).reshape(lengths)]
    another operation x8 -> x0, matrix products: 6.27 us -> none  [gram_solve(): return jax.scipy.linalg.cho_solve((factor_low, True), right_side)]
  transfers between devices with their start and end apart: 4 -> 0, of which waited for: 2 -> 0; matrix products, arithmetic and copies ran while one was open for 13% -> 0% of each run, Pallas kernels for 0% -> 0%
where the time goes in v1:
time: 99.9 us; the launch traced here: 99.7 us
  Pallas kernels  94.8 us (95%)
  local copies, waits for them, and re-layouts  4.28 us (4%)
    pallas_call x1, Pallas kernels, body(): pl.pallas_call(kernel, out_shape=(jax.ShapeDtypeStruct((K, S), f32), jax....  94.8 us
    unnamed x6, local copies, waits for them, and re-layouts  4.28 us

profile of v1, /device:TPU:1, one launch (start us, length us, event | category | flops | bytes accessed | tf_op | source)
XLA Modules:
  0.0 99.7 jit_solution(16813229413405210284)
XLA Ops:
  0.6 0.0 copy-start
  0.6 1.9 %copy-done = bf16[1024,1536]{1,0:T(8,128)(2,1)S(1)} copy-done((bf16[1024,1536]{1,0:T(8,128)(2,1)S(1)}, bf16[1024,1536]{1,0:T(8,128)(2,1)}, u32[]{:S(2)}) %copy-start) | copy-done | bytes 3145752
  2.5 0.0 copy-start.1
  2.5 0.9 copy-done.1
  3.5 94.8 %shard_map.41 = (f32[64,1024]{1,0:T(8,128)S(1)}, f32[64,1536]{1,0:T(8,128)S(1)}) custom-call(bf16[1024,1536]{1,0:T(8,128)(2,1)S(1)} %copy-done, f32[64,1024]{1,0:T(8,128)S(1)} %copy-done.1), custom_call_target="tpu_custom_call" | custom-call | tf_op jit(solution)/shard_map/pallas_call | solution.py:344
  98.2 0.7 copy.6
  98.9 0.7 copy.7
Async XLA Ops:
  0.6 1.9 %copy-start = (bf16[1024,1536]{1,0:T(8,128)(2,1)S(1)}, bf16[1024,1536]{1,0:T(8,128)(2,1)}, u32[]{:S(2)}) copy-start(bf16[1024,1536]{1,0:T(8,128)(2,1)} %g_ref.1) | copy-start | bytes 9437188
  2.5 0.9 copy-start.1
